TPU v7x, 512 devices: a whole 4x4x16 slice. The times are simulated.
512 devices in a mesh: expert: 64 (over z_lo, y, core), dp: 8 (over z_hi, x).
Axes of the slice: x: 4, y: 4, z: 16 (z_hi: 2, z_lo: 8; z = z_hi * 8 + z_lo), core: 2. Of those that a mesh axis runs over, the one named last changes fastest.
Arguments:
- tokens_one: bfloat16 [1536, 4096], P('expert', 'dp'), may hold values from -6 to 6
- gates_one: float32 [1536, 8], P('expert'), may hold values from 0.05 to 1
- experts_one: int32 [1536, 8], P('expert'), may hold values from 0 to 63, all different within a row; in each aligned block of 24 rows (0 to 23, 24 to 47, ...) at most 6 rows name the same one
- tokens_two: bfloat16 [1536, 4096], P('expert', 'dp'), may hold values from -6 to 6
- gates_two: float32 [1536, 8], P('expert'), may hold values from 0.05 to 1
- experts_two: int32 [1536, 8], P('expert'), may hold values from 0 to 63, all different within a row; in each aligned block of 24 rows (0 to 23, 24 to 47, ...) at most 6 rows name the same one
- gate_weight: bfloat16 [64, 1536, 4096], P('expert', 'dp'), may hold values from -0.09375 to 0.09375
- up_weight: bfloat16 [64, 1536, 4096], P('expert', 'dp'), may hold values from -0.09375 to 0.09375
- down_weight: bfloat16 [64, 1536, 4096], P('expert', None, 'dp'), may hold values from -0.15625 to 0.15625
Outputs:
- mixed_one: bfloat16 [1536, 4096], P('expert', 'dp')
- mixed_two: bfloat16 [1536, 4096], P('expert', 'dp')
Inputs may be any that keep to these rules, and one draw needn't show every extreme that they name: `experts_one`: within the rows of one device (24 tokens, aligned blocks) no expert is picked more than 6 times, and each token picks 8 different experts. `experts_two`: within the rows of one device (24 tokens, aligned blocks) no expert is picked more than 6 times, and each token picks 8 different experts.
All inputs are finite; a program needn't handle non-finite values.
Results may differ from a plain program's by a relative error of at most 0.0057.
Values may be sent and summed in bfloat16 or wider, within the bound.
A program may use at most 64 MiB of HBM per device.

v0:
```python
import jax
import jax.numpy as jnp
from jax import lax
from jax.sharding import PartitionSpec as P


def place_rows(expert_ids, expert_count, capacity):
    flat_ids = expert_ids.reshape(-1)
    matches = (flat_ids[:, None] == jnp.arange(expert_count, dtype=jnp.int32)[None, :]).astype(
        jnp.int32
    )
    earlier = jnp.cumsum(matches, axis=0) - matches
    position = jnp.sum(earlier * matches, axis=1)
    slot_ids = flat_ids * capacity + position
    return slot_ids.reshape(expert_ids.shape)


def route_tables(slot_ids, gate_values, slot_total):
    labels = jnp.arange(slot_total, dtype=jnp.int32)
    matches = slot_ids[None, :, :] == labels[:, None, None]
    select = jnp.any(matches, axis=2).astype(jnp.bfloat16)
    weighting = jnp.sum(jnp.where(matches, gate_values[None, :, :], 0.0), axis=2)
    return (select, weighting)


def combine(weighting, returned):
    return jnp.einsum(
        "st,sd->td", weighting, returned.astype(jnp.float32), precision=lax.Precision.HIGHEST
    )


def project_rows(rows, weight_block):
    return lax.dot_general(
        rows, weight_block, (((1,), (1,)), ((), ())), preferred_element_type=jnp.float32
    )


def expert_apply(rows_in, weights):
    gate_w, up_w, down_w = weights
    gate_sum = project_rows(rows_in, gate_w)
    up_sum = project_rows(rows_in, up_w)
    hidden = (jax.nn.silu(gate_sum) * up_sum).astype(jnp.bfloat16)
    result = jnp.dot(
        lax.all_gather(hidden, "dp", axis=1, tiled=True), down_w, preferred_element_type=jnp.float32
    )
    return result.astype(jnp.bfloat16)


def body(
    tokens_one,
    gates_one,
    experts_one,
    tokens_two,
    gates_two,
    experts_two,
    gate_weight,
    up_weight,
    down_weight,
):
    expert_count = lax.axis_size("expert")
    tok_rows, pick_count = experts_one.shape
    capacity = max(2, 2 * tok_rows * pick_count // expert_count)
    slot_total = expert_count * capacity
    weights = (gate_weight[0], up_weight[0], down_weight[0])

    def prepare(tokens):
        return lax.all_gather(tokens, "dp", axis=1, tiled=True)

    def dispatch(rows_in, gate_values, expert_ids):
        slot_ids = place_rows(expert_ids, expert_count, capacity)
        select, weighting = route_tables(slot_ids, gate_values, slot_total)
        outgoing = jnp.dot(select, rows_in, preferred_element_type=jnp.float32).astype(jnp.bfloat16)
        arrived = lax.all_to_all(
            outgoing.reshape(expert_count, capacity, -1),
            "expert",
            split_axis=0,
            concat_axis=0,
            tiled=True,
        )
        produced = expert_apply(arrived.reshape(slot_total, -1), weights)
        returned = lax.all_to_all(
            produced.reshape(expert_count, capacity, -1),
            "expert",
            split_axis=0,
            concat_axis=0,
            tiled=True,
        )
        return combine(weighting, returned.reshape(slot_total, -1))

    mixed_one = dispatch(prepare(tokens_one), gates_one, experts_one).astype(jnp.bfloat16)
    mixed_two = dispatch(prepare(tokens_two), gates_two, experts_two).astype(jnp.bfloat16)
    return (mixed_one, mixed_two)


def solution(mesh):
    return jax.shard_map(
        body,
        mesh=mesh,
        in_specs=(
            P("expert", "dp"),
            P("expert", None),
            P("expert", None),
            P("expert", "dp"),
            P("expert", None),
            P("expert", None),
            P("expert", "dp", None),
            P("expert", "dp", None),
            P("expert", None, "dp"),
        ),
        out_specs=(P("expert", "dp"), P("expert", "dp")),
        check_vma=False,
    )
```

profile of v0, /device:TPU:1, one launch (start us, length us, event | category | flops | bytes accessed | tf_op | source)
XLA Modules:
  0.0 725.3 jit_solution(10441261227321892366)
XLA Ops:
  7.2 0.9 copy.30
  8.1 0.1 eq.80
  8.2 0.6 reduce-window.16
  8.8 0.2 slice_reduce_fusion
  9.0 0.1 bitcast_bitcast_fusion
  9.2 0.1 reduce_sum.44
  9.3 0.2 fusion.30
  9.4 61.8 %all_gather.14 = bf16[24,4096]{1,0:T(8,128)(2,1)S(1)} all-gather(bf16[24,512]{1,0:T(8,128)(2,1)} %param.12), channel_id=1, replica_groups=mesh['expert'=64,'dp'=8] {'dp'}, dimensions={1}, use_global_device_ids=true | all-gather | bytes 221184 | tf_op jit(solution)/shard_map/all_gather | solution.py:67
  71.3 2.7 convolution_convert_fusion
  73.9 5.6 reshape.76
  79.6 19.1 %all-to-all-start.2 = ((bf16[64,6,4096]{2,1,0:T(8,128)(2,1)}), bf16[64,6,4096]{2,1,0:T(8,128)(2,1)}, u32[]{:S(2)}, u32[]{:S(2)}) async-start(bf16[64,6,4096]{2,1,0:T(8,128)(2,1)} %reshape.76), calls=%async_computation.2 | async-start | bytes 8388608 | tf_op jit(solution)/shard_map/all_to_all | solution.py:73
  98.7 0.1 copy.25
  98.8 0.1 eq.70
  98.9 0.6 reduce-window.14
  99.6 0.2 slice_reduce_fusion.1
  99.8 0.1 bitcast_bitcast_fusion.1
  99.9 0.1 reduce_sum.41
  100.0 131.9 %all_gather.12 = bf16[24,4096]{1,0:T(8,128)(2,1)S(1)} all-gather(bf16[24,512]{1,0:T(8,128)(2,1)S(1)} %copy-done.3), channel_id=1, replica_groups=mesh['expert'=64,'dp'=8] {'dp'}, dimensions={1}, use_global_device_ids=true | all-gather | bytes 221184 | tf_op jit(solution)/shard_map/all_gather | solution.py:67
  232.0 0.2 fusion.31
  232.1 2.7 convolution_convert_fusion.1
  234.8 5.6 reshape.70
  240.5 50.0 %all-to-all-done.2 = bf16[64,6,4096]{2,1,0:T(8,128)(2,1)} async-done(((bf16[64,6,4096]{2,1,0:T(8,128)(2,1)}), bf16[64,6,4096]{2,1,0:T(8,128)(2,1)}, u32[]{:S(2)}, u32[]{:S(2)}) %all-to-all-start.2) | async-done | bytes 3145760 | tf_op jit(solution)/shard_map/all_to_all | solution.py:73
  290.4 59.8 %all-to-all-start = ((bf16[64,6,4096]{2,1,0:T(8,128)(2,1)}), bf16[64,6,4096]{2,1,0:T(8,128)(2,1)}, u32[]{:S(2)}, u32[]{:S(2)}) async-start(bf16[64,6,4096]{2,1,0:T(8,128)(2,1)} %reshape.70), calls=%async_computation | async-start | bytes 8388608 | tf_op jit(solution)/shard_map/all_to_all | solution.py:73
  350.3 5.7 reshape.77
  356.0 3.7 fusion.8
  359.7 0.1 copy-done.7
  359.8 1.9 fusion.24
  361.7 205.8 %all-to-all-done = bf16[64,6,4096]{2,1,0:T(8,128)(2,1)} async-done(((bf16[64,6,4096]{2,1,0:T(8,128)(2,1)}), bf16[64,6,4096]{2,1,0:T(8,128)(2,1)}, u32[]{:S(2)}, u32[]{:S(2)}) %all-to-all-start) | async-done | bytes 3145760 | tf_op jit(solution)/shard_map/all_to_all | solution.py:73
  567.5 5.7 reshape.71
  573.3 3.7 fusion.10
  577.0 0.1 copy-done.8
  577.0 1.9 fusion.27
  578.9 2.1 fusion.15
  581.0 0.9 reshape.78
  582.0 8.4 %all-to-all-start.3 = ((bf16[64,6,512]{2,1,0:T(8,128)(2,1)}), bf16[64,6,512]{2,1,0:T(8,128)(2,1)S(1)}, u32[]{:S(2)}, u32[]{:S(2)}) async-start(bf16[64,6,512]{2,1,0:T(8,128)(2,1)} %reshape.78), calls=%async_computation.3 | async-start | bytes 1048576 | tf_op jit(solution)/shard_map/all_to_all | solution.py:81
  590.4 86.5 %all-gather.3.cloned.1.call-done = bf16[384,1536]{0,1:T(8,128)(2,1)} async-done(((bf16[384,192]{0,1:T(8,128)(2,1)}), bf16[384,1536]{0,1:T(8,128)(2,1)}) %all-gather.3.cloned.1.call-update) | async-done | bytes 1179664 | tf_op jit(solution)/shard_map/all_gather | solution.py:44
  676.9 2.1 fusion.12
  679.0 0.9 reshape.72
  679.9 7.3 %all-to-all-start.1 = ((bf16[64,6,512]{2,1,0:T(8,128)(2,1)}), bf16[64,6,512]{2,1,0:T(8,128)(2,1)S(1)}, u32[]{:S(2)}, u32[]{:S(2)}) async-start(bf16[64,6,512]{2,1,0:T(8,128)(2,1)} %reshape.72), calls=%async_computation.1 | async-start | bytes 1048576 | tf_op jit(solution)/shard_map/all_to_all | solution.py:81
  687.3 0.1 copy.34
  687.3 0.1 copy.29
  687.4 0.2 select_reduce_fusion
  687.6 0.2 select_reduce_fusion.1
  687.8 0.1 reshape.79
  687.9 0.9 convolution_convert_fusion.2
  688.8 28.6 %all-to-all-done.1 = bf16[64,6,512]{2,1,0:T(8,128)(2,1)S(1)} async-done(((bf16[64,6,512]{2,1,0:T(8,128)(2,1)}), bf16[64,6,512]{2,1,0:T(8,128)(2,1)S(1)}, u32[]{:S(2)}, u32[]{:S(2)}) %all-to-all-start.1) | async-done | bytes 393248 | tf_op jit(solution)/shard_map/all_to_all | solution.py:81
  717.4 0.1 reshape.73
  717.6 0.9 convolution_convert_fusion.3
  (34 shorter events, 0.4 us)
Async XLA Ops:
  7.2 571.8 %copy-start = (bf16[1,1536,512]{2,1,0:T(8,128)(2,1)S(1)}, bf16[1,1536,512]{2,1,0:T(8,128)(2,1)}, u32[]{:S(2)}) copy-start(bf16[1,1536,512]{2,1,0:T(8,128)(2,1)} %param.17) | copy-start | bytes 4718596
  79.6 19.1 %copy-start.4 = (s32[24,8]{0,1:T(8,128)S(1)}, s32[24,8]{0,1:T(8,128)}, u32[]{:S(2)}) copy-start(s32[24,8]{0,1:T(8,128)} %param.11) | copy-start | bytes 2308
  79.6 20.4 %copy-start.3 = (bf16[24,512]{1,0:T(8,128)(2,1)S(1)}, bf16[24,512]{1,0:T(8,128)(2,1)}, u32[]{:S(2)}) copy-start(bf16[24,512]{1,0:T(8,128)(2,1)} %param.9) | copy-start | bytes 73732
  79.6 210.8 %all-to-all-start.2 = ((bf16[64,6,4096]{2,1,0:T(8,128)(2,1)}), bf16[64,6,4096]{2,1,0:T(8,128)(2,1)}, u32[]{:S(2)}, u32[]{:S(2)}) async-start(bf16[64,6,4096]{2,1,0:T(8,128)(2,1)} %reshape.76), calls=%async_computation.2 | async-start | bytes 8388608 | tf_op jit(solution)/shard_map/all_to_all | solution.py:73
  290.4 277.1 %all-to-all-start = ((bf16[64,6,4096]{2,1,0:T(8,128)(2,1)}), bf16[64,6,4096]{2,1,0:T(8,128)(2,1)}, u32[]{:S(2)}, u32[]{:S(2)}) async-start(bf16[64,6,4096]{2,1,0:T(8,128)(2,1)} %reshape.70), calls=%async_computation | async-start | bytes 8388608 | tf_op jit(solution)/shard_map/all_to_all | solution.py:73
  350.2 228.7 %all-gather.5.cloned.1.call-start = ((), (), s32[]{:S(2)}) async-start(), calls=%async_computation.5 | async-start | bytes 1327104 | tf_op jit(solution)/shard_map/all_gather | solution.py:44
  356.0 3.7 copy-start.1
  356.0 3.8 copy-start.7
  361.6 315.3 %all-gather.3.cloned.1.call-start = ((), (), s32[]{:S(2)}) async-start(), calls=%async_computation.4 | async-start | bytes 1327104 | tf_op jit(solution)/shard_map/all_gather | solution.py:44
  573.2 3.7 copy-start.2
  573.3 3.8 copy-start.8
  582.0 98.0 %all-to-all-start.3 = ((bf16[64,6,512]{2,1,0:T(8,128)(2,1)}), bf16[64,6,512]{2,1,0:T(8,128)(2,1)S(1)}, u32[]{:S(2)}, u32[]{:S(2)}) async-start(bf16[64,6,512]{2,1,0:T(8,128)(2,1)} %reshape.78), calls=%async_computation.3 | async-start | bytes 1048576 | tf_op jit(solution)/shard_map/all_to_all | solution.py:81
  679.0 8.3 %copy-start.5 = (f32[24,8]{0,1:T(8,128)S(1)}, f32[24,8]{0,1:T(8,128)}, u32[]{:S(2)}) copy-start(f32[24,8]{0,1:T(8,128)} %param.13) | copy-start | bytes 2308
  679.0 8.3 %copy-start.6 = (f32[24,8]{0,1:T(8,128)S(1)}, f32[24,8]{0,1:T(8,128)}, u32[]{:S(2)}) copy-start(f32[24,8]{0,1:T(8,128)} %param.10) | copy-start | bytes 2308
  679.9 37.5 %all-to-all-start.1 = ((bf16[64,6,512]{2,1,0:T(8,128)(2,1)}), bf16[64,6,512]{2,1,0:T(8,128)(2,1)S(1)}, u32[]{:S(2)}, u32[]{:S(2)}) async-start(bf16[64,6,512]{2,1,0:T(8,128)(2,1)} %reshape.72), calls=%async_computation.1 | async-start | bytes 1048576 | tf_op jit(solution)/shard_map/all_to_all | solution.py:81
Sparse Core Ops, SparseCore 0:
  361.8 112.4 all-gather.4
  579.0 97.8 all-gather.2
where the time goes:
time: 726 us; the launch traced here: 725 us
  waiting for transfers between devices  371 us (51%)
  blocking collectives  194 us (27%)
  starting transfers between devices  94.7 us (13%)
  local copies, waits for them, and re-layouts  26.9 us (4%)
  matrix products  22.4 us (3%)
  between operations  14.3 us (2%)
    all_to_all x2, waiting for transfers between devices, dispatch(): lax.all_to_all(outgoing.reshape(expert_count, capacity, -1), 'expert', sp...  256 us
    all_gather x2, blocking collectives, prepare(): return lax.all_gather(tokens, 'dp', axis=1, tiled=True)  194 us
    all_gather x2, waiting for transfers between devices, expert_apply(): lax.all_gather(hidden, 'dp', axis=1, tiled=True)  86.5 us
    all_to_all x2, starting transfers between devices, dispatch(): lax.all_to_all(outgoing.reshape(expert_count, capacity, -1), 'expert', sp...  78.9 us
    all_to_all x2, waiting for transfers between devices, dispatch(): lax.all_to_all(produced.reshape(expert_count, capacity, -1), 'expert', sp...  28.6 us
    all_to_all x2, starting transfers between devices, dispatch(): lax.all_to_all(produced.reshape(expert_count, capacity, -1), 'expert', sp...  15.7 us
  transfers between devices with their start and end apart: 6, of which 4 were waited for; matrix products, arithmetic and copies ran while one was open for 5% of the time, Pallas kernels for 0%

commit v1 on v0

v1 whole, which is shorter than its diff:
```python
import jax
import jax.numpy as jnp
from jax import lax
from jax.experimental import pallas as pl
from jax.experimental.pallas import tpu as pltpu
from jax.sharding import PartitionSpec as P

MESH = pl.DeviceIdType.MESH
BF16, F32 = jnp.bfloat16, jnp.float32
NT = (((1,), (1,)), ((), ()))
TN = (((0,), (0,)), ((), ()))

TOK = 24
BOTH = 2 * TOK
CAP = 6
SLOTS = 8 * CAP
ROWS = 8 * SLOTS
HID = 192
WID = 512
COPIES = 84
ALL = 8 * BOTH


def dot(a, b, dims=(((1,), (0,)), ((), ()))):
    return lax.dot_general(a, b, dims, preferred_element_type=F32)


def iota(shape, axis):
    return lax.broadcasted_iota(jnp.int32, shape, axis)


def kernel(
    tok1, gat1, exp1, tok2, gat2, exp2, gate_w, up_w, down_w,
    out1, out2,
    ZT, IG, SM, YS, SEL, WX, DW, PS, PR, PO, HT, OA, OS, OB, CM, ZF, ZS, ZR,
    ssem, rsem, lsem,
):
    e, d = lax.axis_index("expert"), lax.axis_index("dp")
    zh, x = d // 4, lax.rem(d, 4)
    zl, i8 = e // 8, lax.rem(e, 8)
    z = zh * 8 + zl
    ql = zl // 4
    q = zh * 2 + ql

    def at_z(step):
        other = lax.rem(z + step + 16, 16)
        return (lax.rem(other, 8) * 8 + i8, (other // 8) * 4 + x)

    def at_zl(step):
        return (lax.rem(zl + step + 8, 8) * 8 + i8, d)

    def at_x(step):
        return (e, zh * 4 + lax.rem(x + step + 4, 4))

    def at_yc(step):
        return (zl * 8 + lax.rem(i8 + step + 8, 8), d)

    barrier = pltpu.get_barrier_semaphore()
    greeted = (
        [at_z(k) for k in range(1, 16)]
        + [at_x(k) for k in range(1, 4)]
        + [at_yc(k) for k in range(1, 8)]
    )
    for who in greeted:
        pl.semaphore_signal(barrier, inc=1, device_id=who, device_id_type=MESH)

    copies = []

    def send(src, dst, who):
        n = len(copies)
        copy = pltpu.make_async_remote_copy(
            src_ref=src,
            dst_ref=dst,
            send_sem=ssem.at[n],
            recv_sem=rsem.at[n],
            device_id=who,
            device_id_type=MESH,
        )
        copy.start()
        copies.append(copy)
        return copy

    local = []

    def fetch(src, dst):
        copy = pltpu.make_async_copy(src, dst, lsem.at[len(local)])
        copy.start()
        local.append(copy)

    def columns(half, owner):
        return pl.ds(pl.multiple_of(half * 2048 + owner * WID, WID), WID)

    for half in range(2):
        for n, w in enumerate((gate_w, up_w)):
            fetch(
                w.at[0, :, columns(half, x)],
                WX.at[0, pl.ds(n * HID, HID), pl.ds(half * WID, WID)],
            )
    fetch(down_w.at[0], DW)

    ZT[0, q] = jnp.concatenate([tok1[...].astype(F32), tok2[...].astype(F32)], axis=0).astype(BF16)
    lane = iota((TOK, 128), 1)
    tables = []
    for gates, experts in ((gat1, exp1), (gat2, exp2)):
        table = jnp.zeros((TOK, 128), F32)
        for k in range(8):
            hit = lax.rem(lane, 64) == experts[:, k : k + 1]
            table = jnp.where(hit, gates[:, k : k + 1], table)
        high = table.astype(BF16).astype(F32)
        tables.append(jnp.where(lane < 64, high, table - high))
    IG[0, ql] = jnp.concatenate(tables, axis=0).astype(BF16)

    pl.semaphore_wait(barrier, len(greeted))

    first = [send(ZT.at[0, q], ZT.at[0, q], at_z(4 * a)) for a in (1, 2, 3)]
    first.append(send(IG.at[0, ql], IG.at[0, ql], at_z(4)))
    weights = []
    for k in (1, 3, 2):
        owner = lax.rem(x + k, 4)
        for half in range(2):
            for n, w in enumerate((gate_w, up_w)):
                weights.append(
                    send(
                        w.at[0, :, columns(half, owner)],
                        WX.at[k, pl.ds(n * HID, HID), pl.ds(half * WID, WID)],
                        at_x(k),
                    )
                )

    for copy in first:
        copy.wait_recv()
    second = []
    for b, step in ((1, -1), (3, 1), (2, 2)):
        second.append(send(IG.at[0], IG.at[b], at_z(step)))
        second.append(send(ZT.at[0], ZT.at[b], at_z(step)))

    rows, cols = iota((ALL, ALL), 0), iota((ALL, ALL), 1)
    block = rows // TOK == cols // TOK
    before = jnp.where(block & (rows < cols), 1.0, 0.0).astype(BF16)
    after = jnp.where(block & (cols < rows), 1.0, 0.0).astype(BF16)
    pick, lane = iota((128, 128), 0), iota((128, 128), 1)
    wanted = zl * 8 + lax.rem(i8 + pick, 8)
    picks = jnp.where(
        ((pick < 8) & (lane == wanted)) | ((pick >= 8) & (pick < 16) & (lane == wanted + 64)),
        1.0,
        0.0,
    ).astype(BF16)

    for copy in second:
        copy.wait_recv()

    info = IG[...].reshape(ALL, 128)
    chosen = dot(picks[:16], info, NT)
    taken = chosen > 0.0
    place = dot(jnp.where(taken, 1.0, 0.0).astype(BF16), before)
    token = iota((16, ALL), 1)
    slot = place.astype(jnp.int32) + token // BOTH * CAP
    step_of = lax.rem(token, BOTH) // TOK
    for s in range(2):
        aim = jnp.where(taken & (step_of == s), slot, -1)
        for k in range(8):
            SM[s, k * SLOTS : (k + 1) * SLOTS] = jnp.where(
                iota((SLOTS, ALL), 0) == aim[k : k + 1], 1.0, 0.0
            ).astype(BF16)
    dispatch = []
    for s in range(2):
        for half in range(2):
            held = jnp.concatenate(
                [ZT[b, 2 * half : 2 * half + 2].reshape(2 * BOTH, WID) for b in range(4)], axis=0
            )
            YS[s, :, half * WID : (half + 1) * WID] = dot(SM[s], held).astype(BF16)
        dispatch.append(
            [
                send(YS.at[s, pl.ds(k * SLOTS, SLOTS)], SEL.at[s, pl.ds(k * SLOTS, SLOTS)], at_yc(k))
                for k in range(1, 8)
            ]
        )
        SEL[s, 0:SLOTS] = YS[s, 0:SLOTS]

    gates = dot(info, picks, NT)
    count = dot(after, jnp.where(gates > 0.0, 1.0, 0.0).astype(BF16))
    base = (iota((ALL, 128), 0) // BOTH * CAP + iota((ALL, 128), 1) * SLOTS).astype(F32)
    target = jnp.where(gates > 0.0, count + base, -1.0)
    column = iota((8 * TOK, ROWS), 1).astype(F32)
    for s in range(2):
        part = lambda v: v.reshape(8, BOTH, 128)[:, s * TOK : (s + 1) * TOK].reshape(8 * TOK, 128)
        aim, value = part(target), part(gates)
        for n in range(2):
            total = jnp.zeros((8 * TOK, ROWS), F32)
            for k in range(8):
                hit = column == aim[:, k : k + 1]
                total = jnp.where(hit, value[:, 8 * n + k : 8 * n + k + 1], total)
            CM[s, n] = total.astype(BF16)

    for copy in local:
        copy.wait()
    partial = []
    for s in range(2):
        for copy in dispatch[s]:
            copy.wait_recv()
        sent = []
        for n, k in enumerate((1, 3, 2)):
            if s == 0:
                for copy in weights[4 * n : 4 * n + 4]:
                    copy.wait_recv()
            PS[s, k] = dot(WX[k], SEL[s], NT).astype(BF16)
            sent.append(send(PS.at[s, k], PR.at[s, k], at_x(-k)))
        PO[s] = dot(WX[0], SEL[s], NT)
        partial.append(sent)

    crossed, around, forwarded = [], [], []
    for s in range(2):
        for copy in partial[s]:
            copy.wait_recv()
        both = PO[s]
        for k in range(1, 4):
            both = both + PR[s, k].astype(F32)
        gate, up = both[:HID], both[HID:]
        HT[s, d] = (gate / (1.0 + jnp.exp(-gate)) * up).astype(BF16)
        crossed.append(send(HT.at[s, d], HT.at[s, d], at_z(8)))
        around.append([send(HT.at[s, d], HT.at[s, d], at_x(k)) for k in (1, 3, 2)])

    other = lax.rem(d + 4, 8)

    def pass_on(s):
        crossed[s].wait_recv()
        forwarded.append([send(HT.at[s, other], HT.at[s, other], at_x(k)) for k in (1, 3, 2)])

    returned = []

    def project(s):
        for copy in around[s] + forwarded[s]:
            copy.wait_recv()
        OA[...] = jnp.zeros((ROWS, WID), F32)

        @pl.loop(0, 8)
        def _(n):
            w = DW[pl.ds(pl.multiple_of(n * HID, HID), HID), :]
            OA[...] += dot(HT[s, n], w, TN)

        OS[s] = OA[...].astype(BF16)
        returned.append(
            [
                send(OS.at[s, pl.ds(k * SLOTS, SLOTS)], OB.at[s, pl.ds(k * SLOTS, SLOTS)], at_yc(-k))
                for k in range(1, 8)
            ]
        )
        OB[s, 0:SLOTS] = OS[s, 0:SLOTS]

    last = []

    def combine(s):
        for copy in returned[s]:
            copy.wait_recv()
        rows_in = OB[s]
        total = (dot(CM[s, 0], rows_in) + dot(CM[s, 1], rows_in)).reshape(8, TOK, WID)
        for n in range(4):
            ZF[s, :, n * TOK : (n + 1) * TOK] = total[:, :, n * 128 : (n + 1) * 128]
        ZS[s] = ZF[s].astype(BF16)
        sent = []
        for k in range(1, 8):
            block = k % 4 * 2 + lax.rem(zl + k, 8) // 4
            sent.append(send(ZS.at[s, block], ZR.at[s, k], at_zl(k)))
        last.append(sent)

    def finish(s, out):
        for copy in last[s]:
            copy.wait_recv()
        total = ZF[s, ql]
        for k in range(1, 8):
            total = total + ZR[s, k].astype(F32)
        for n in range(4):
            out[:, n * 128 : (n + 1) * 128] = total[n * TOK : (n + 1) * TOK].astype(BF16)

    pass_on(0)
    project(0)
    pass_on(1)
    combine(0)
    project(1)
    combine(1)
    finish(0, out1)
    finish(1, out2)
    for copy in copies:
        copy.wait_send()


def body(tok1, gat1, exp1, tok2, gat2, exp2, gate_w, up_w, down_w):
    vmem = pl.BlockSpec(memory_space=pltpu.VMEM)
    hbm = pl.BlockSpec(memory_space=pl.ANY)
    scratch = [
        pltpu.VMEM((4, 4, BOTH, WID), BF16),
        pltpu.VMEM((4, 2, BOTH, 128), BF16),
        pltpu.VMEM((2, ROWS, ALL), BF16),
        pltpu.VMEM((2, ROWS, 2 * WID), BF16),
        pltpu.VMEM((2, ROWS, 2 * WID), BF16),
        pltpu.VMEM((4, 2 * HID, 2 * WID), BF16),
        pltpu.VMEM((8 * HID, WID), BF16),
        pltpu.VMEM((2, 4, 2 * HID, ROWS), BF16),
        pltpu.VMEM((2, 4, 2 * HID, ROWS), BF16),
        pltpu.VMEM((2, 2 * HID, ROWS), F32),
        pltpu.VMEM((2, 8, HID, ROWS), BF16),
        pltpu.VMEM((ROWS, WID), F32),
        pltpu.VMEM((2, ROWS, WID), BF16),
        pltpu.VMEM((2, ROWS, WID), BF16),
        pltpu.VMEM((2, 2, 8 * TOK, ROWS), BF16),
        pltpu.VMEM((2, 8, 4 * TOK, 128), F32),
        pltpu.VMEM((2, 8, 4 * TOK, 128), BF16),
        pltpu.VMEM((2, 8, 4 * TOK, 128), BF16),
        pltpu.SemaphoreType.DMA((COPIES,)),
        pltpu.SemaphoreType.DMA((COPIES,)),
        pltpu.SemaphoreType.DMA((5,)),
    ]
    result = jax.ShapeDtypeStruct((TOK, WID), BF16)
    return pl.pallas_call(
        kernel,
        out_shape=(result, result),
        in_specs=[vmem] * 6 + [hbm] * 3,
        out_specs=(vmem, vmem),
        scratch_shapes=scratch,
        compiler_params=pltpu.CompilerParams(
            collective_id=0, has_side_effects=True, vmem_limit_bytes=48 * 2**20
        ),
        cost_estimate=pl.CostEstimate(
            flops=2 * 2 * ROWS * (2 * HID * 4096 + 1536 * WID),
            bytes_accessed=3 * HID * 4096 * 2,
            transcendentals=2 * HID * ROWS,
        ),
        name="moe",
    )(tok1, gat1, exp1, tok2, gat2, exp2, gate_w, up_w, down_w)


def solution(mesh):
    return jax.shard_map(
        body,
        mesh=mesh,
        in_specs=(
            P("expert", "dp"),
            P("expert", None),
            P("expert", None),
            P("expert", "dp"),
            P("expert", None),
            P("expert", None),
            P("expert", "dp", None),
            P("expert", "dp", None),
            P("expert", None, "dp"),
        ),
        out_specs=(P("expert", "dp"), P("expert", "dp")),
        check_vma=False,
    )
```

time: 726 us -> 144 us (0.20)
  waiting for transfers between devices: 371 us -> 0 us
  blocking collectives: 194 us -> 0 us
  Pallas kernels: 0 us -> 133 us
  starting transfers between devices: 94.7 us -> 0 us
  matrix products: 22.4 us -> 0 us
  local copies, waits for them, and re-layouts: 26.9 us -> 9.95 us
  between operations: 14.3 us -> 0.65 us
    all_to_all x4 -> x0, waiting for transfers between devices: 284 us -> none  [the longest x2 256 us: dispatch(): lax.all_to_all(outgoing.reshape(expert_count, capacity, -1), 'expert', sp...]
    all_gather x2 -> x0, blocking collectives: 194 us -> none  [prepare(): return lax.all_gather(tokens, 'dp', axis=1, tiled=True)]
    pallas_call x0 -> x1, Pallas kernels: none -> 133 us  [body(): pl.pallas_call(kernel, out_shape=(result, result), in_specs=[vmem] * 6 +...]
    all_to_all x4 -> x0, starting transfers between devices: 94.6 us -> none  [the longest x2 78.9 us: dispatch(): lax.all_to_all(outgoing.reshape(expert_count, capacity, -1), 'expert', sp...]
    all_gather x2 -> x0, waiting for transfers between devices: 86.5 us -> none  [expert_apply(): lax.all_gather(hidden, 'dp', axis=1, tiled=True)]
    reshape x8 -> x0, local copies, waits for them, and re-layouts: 24.9 us -> none  [the longest x2 11.4 us: dispatch(): produced = expert_apply(arrived.reshape(slot_total, -1), weights)]
    dot_general x10 -> x0, matrix products: 22.4 us -> none  [the longest x4 11.1 us: project_rows(): lax.dot_general(rows, weight_block, (((1,), (1,)), ((), ())), preferred_e...]
    unnamed x22 -> x16, local copies, waits for them, and re-layouts: 1.28 us -> 9.95 us
  transfers between devices with their start and end apart: 6 -> 0, of which waited for: 4 -> 0; matrix products, arithmetic and copies ran while one was open for 5% -> 0% of each run, Pallas kernels for 0% -> 0%
where the time goes in v1:
time: 144 us; the launch traced here: 143 us
  Pallas kernels  133 us (92%)
  local copies, waits for them, and re-layouts  9.95 us (7%)
    pallas_call x1, Pallas kernels, body(): pl.pallas_call(kernel, out_shape=(result, result), in_specs=[vmem] * 6 +...  133 us
    unnamed x16, local copies, waits for them, and re-layouts  9.95 us

profile of v1, /device:TPU:1, one launch (start us, length us, event | category | flops | bytes accessed | tf_op | source)
XLA Modules:
  0.0 143.1 jit_solution(2389090083711149288)
XLA Ops:
  0.6 0.8 copy.11.gat1
  1.4 0.8 copy.12.exp1
  2.1 0.8 copy.13.gat2
  2.9 0.8 copy.14.exp2
  3.7 0.0 copy-start
  3.7 1.4 copy-done
  5.1 0.0 copy-start.1
  5.1 1.4 copy-done.1
  6.5 0.0 copy-start.2
  6.5 1.4 copy-done.2
  7.9 0.0 copy-start.3
  7.9 0.7 copy-done.3
  8.6 0.0 copy-start.4
  8.6 0.7 copy-done.4
  9.4 132.5 %moe.1 = (bf16[24,512]{1,0:T(8,128)(2,1)S(1)}, bf16[24,512]{1,0:T(8,128)(2,1)S(1)}) custom-call(bf16[24,512]{1,0:T(8,128)(2,1)S(1)} %copy-done.3, f32[24,8]{1,0:T(8,128)S(1)} %copy.11.gat1, s32[24,8]{1,0:T(8,128)S(1)} %copy.12.exp1, bf16[24,512]{1,0:T(8,128)(2,1)S(1)} %copy-done.4, f32[24,8]{1,0:T(8,128)S(1)} %copy.13.gat2, s32[24,8]{1,0:T(8,128)S(1)} %copy.14.exp2, ...), custom_call_target="tpu_custom_call" | custom-call | flops 3623878656 | bytes 4718592 | tf_op jit(solution)/shard_map/moe/pallas_call | solution.py:314
  141.9 0.6 copy.17
  142.5 0.6 copy.18
Async XLA Ops:
  3.7 1.4 copy-start
  5.1 1.4 copy-start.1
  6.5 1.4 copy-start.2
  7.9 0.7 copy-start.3
  8.6 0.7 copy-start.4

commit v2 on v1

v2 whole, which is shorter than its diff:
```python
import jax
import jax.numpy as jnp
from jax import lax
from jax.experimental import pallas as pl
from jax.experimental.pallas import tpu as pltpu
from jax.sharding import PartitionSpec as P

MESH = pl.DeviceIdType.MESH
BF16, F32 = jnp.bfloat16, jnp.float32
NT = (((1,), (1,)), ((), ()))
TN = (((0,), (0,)), ((), ()))

TOK = 24
BOTH = 2 * TOK
CAP = 6
SLOTS = 8 * CAP
ROWS = 8 * SLOTS
HID = 192
WID = 512
COPIES = 127
HEAD = 32
CHUNKS = (((0, 384),), ((0, 256), (256, 384)))
AROUND = ((1, -1), (3, 1), (2, 2))
ALL = 8 * BOTH


def dot(a, b, dims=(((1,), (0,)), ((), ()))):
    return lax.dot_general(a, b, dims, preferred_element_type=F32)


def iota(shape, axis):
    return lax.broadcasted_iota(jnp.int32, shape, axis)


def kernel(
    tok1, gat1, exp1, tok2, gat2, exp2, gate_w, up_w, down_w,
    out1, out2,
    TV, GV, EV, ZT, IG, SM, YS, TK, WO, WA, WB, DW, PS, PR, PO, HT, OA, OS, OB, CM, ZF, ZS, ZR,
    ssem, rsem, lsem,
):
    e, d = lax.axis_index("expert"), lax.axis_index("dp")
    zh, x = d // 4, lax.rem(d, 4)
    zl, i8 = e // 8, lax.rem(e, 8)
    z = zh * 8 + zl
    ql = zl // 4
    q = zh * 2 + ql
    xa, xb, xc = x + 1 - 2 * lax.rem(x, 2), 3 - x, lax.rem(x + 2, 4)

    def at_z(step):
        other = lax.rem(z + step + 16, 16)
        return (lax.rem(other, 8) * 8 + i8, (other // 8) * 4 + x)

    def at_zl(step):
        return (lax.rem(zl + step + 8, 8) * 8 + i8, d)

    def at_x(place):
        return (e, zh * 4 + place)

    def at_yc(step):
        return (zl * 8 + lax.rem(i8 + step + 8, 8), d)

    barrier = pltpu.get_barrier_semaphore()
    greeted = (
        [at_z(k) for k in range(1, 16)]
        + [at_x(place) for place in (xa, xb, xc)]
        + [at_yc(k) for k in range(1, 8)]
    )
    for who in greeted:
        pl.semaphore_signal(barrier, inc=1, device_id=who, device_id_type=MESH)

    local = []

    def fetch(src, dst):
        copy = pltpu.make_async_copy(src, dst, lsem.at[len(local)])
        copy.start()
        local.append(copy)

    def columns(half, owner):
        return pl.ds(pl.multiple_of(half * 2048 + owner * WID, WID), WID)

    for n, (tok, gat, exp) in enumerate(((tok1, gat1, exp1), (tok2, gat2, exp2))):
        fetch(tok, TV.at[n])
        fetch(gat, GV.at[n])
        fetch(exp, EV.at[n])
    for m, cols in enumerate((columns(0, xa), columns(0, x), columns(1, x), columns(1, xb))):
        for n, w in enumerate((gate_w, up_w)):
            fetch(w.at[0, :, cols], WO.at[pl.ds(n * HID, HID), pl.ds(m * WID, WID)])
    fetch(down_w.at[0], DW)

    copies = []

    def send(src, dst, who):
        n = len(copies)
        copy = pltpu.make_async_remote_copy(
            src_ref=src,
            dst_ref=dst,
            send_sem=ssem.at[n],
            recv_sem=rsem.at[n],
            device_id=who,
            device_id_type=MESH,
        )
        copy.start()
        copies.append(copy)
        return copy

    for copy in local[:6]:
        copy.wait()
    ZT[0, q] = jnp.concatenate([TV[0].astype(F32), TV[1].astype(F32)], axis=0).astype(BF16)
    label = iota((128, TOK), 0)
    unit = jnp.where(iota((128, 128), 0) == iota((128, 128), 1), 1.0, 0.0).astype(BF16)
    tables = []
    for s in range(2):
        gates, experts = GV[s], EV[s]
        table = jnp.zeros((128, TOK), F32)
        for k in range(8):
            hit = lax.rem(label, 64) == experts[k : k + 1]
            table = jnp.where(hit, gates[k : k + 1], table)
        high = table.astype(BF16).astype(F32)
        tables.append(dot(jnp.where(label < 64, high, table - high).astype(BF16), unit, TN))
    IG[0, ql] = jnp.concatenate(tables, axis=0).astype(BF16)

    pl.semaphore_wait(barrier, len(greeted))

    parts = (pl.ds(0, HEAD), pl.ds(HEAD, BOTH - HEAD))
    first, second, table_second = {}, ([], []), []

    def spread(n, a):
        block = lax.rem(q - a + 4, 4)
        for b, step in AROUND:
            src = ZT.at[0, block, parts[n]]
            second[n].append(send(src, ZT.at[b, block, parts[n]], at_z(step)))

    table_first = send(IG.at[0, ql], IG.at[0, ql], at_z(4))
    for a in (2, 1, 3):
        first[0, a] = send(ZT.at[0, q, parts[0]], ZT.at[0, q, parts[0]], at_z(4 * a))
    spread(0, 0)
    table_first.wait_recv()
    table_second += [send(IG.at[0], IG.at[b], at_z(step)) for b, step in AROUND]
    for a in (1, 3):
        first[0, a].wait_recv()
        spread(0, a)
    for a in (2, 1, 3):
        first[1, a] = send(ZT.at[0, q, parts[1]], ZT.at[0, q, parts[1]], at_z(4 * a))
    first[0, 2].wait_recv()
    spread(0, 2)
    spread(1, 0)
    weights = []
    for cols, buffer, place in (
        ((columns(1, xa), columns(1, xc)), WA, xa),
        ((columns(0, xc), columns(0, xb)), WB, xb),
    ):
        for m in range(2):
            for h, w in enumerate((gate_w, up_w)):
                dst = buffer.at[pl.ds(h * HID, HID), pl.ds(m * WID, WID)]
                weights.append(send(w.at[0, :, cols[m]], dst, at_x(place)))
    for a in (1, 3, 2):
        first[1, a].wait_recv()
        spread(1, a)

    rows, cols = iota((ALL, ALL), 0), iota((ALL, ALL), 1)
    block = rows // TOK == cols // TOK
    before = jnp.where(block & (rows < cols), 1.0, 0.0).astype(BF16)
    after = jnp.where(block & (cols < rows), 1.0, 0.0).astype(BF16)
    pick, lane = iota((128, 128), 0), iota((128, 128), 1)
    wanted = zl * 8 + lax.rem(i8 + pick, 8)
    picks = jnp.where(
        ((pick < 8) & (lane == wanted)) | ((pick >= 8) & (pick < 16) & (lane == wanted + 64)),
        1.0,
        0.0,
    ).astype(BF16)

    for copy in table_second:
        copy.wait_recv()
    info = IG[...].reshape(ALL, 128)
    chosen = dot(picks[:16], info, NT)
    taken = chosen > 0.0
    place = dot(jnp.where(taken, 1.0, 0.0).astype(BF16), before)
    token = iota((16, ALL), 1)
    slot = place.astype(jnp.int32) + token // BOTH * CAP
    step_of = lax.rem(token, BOTH) // TOK
    held_row, all_row = iota((8 * HEAD, ALL), 0), iota((8 * HEAD, ALL), 1)
    for s in range(2):
        aim = jnp.where(taken & (step_of == s), slot, -1).astype(F32)
        same = held_row // HEAD * BOTH + lax.rem(held_row, HEAD) + s * (BOTH - HEAD) == all_row
        aim = dot(aim.astype(BF16), jnp.where(same, 1.0, 0.0).astype(BF16), NT)
        for k in range(8):
            SM[s, k * SLOTS : (k + 1) * SLOTS] = jnp.where(
                iota((SLOTS, 8 * HEAD), 0).astype(F32) == aim[k : k + 1], 1.0, 0.0
            ).astype(BF16)
    dispatch = []

    def select(s):
        start = s * (BOTH - HEAD)
        for half in range(2):
            held = ZT[:, 2 * half : 2 * half + 2, start : start + HEAD].reshape(8 * HEAD, WID)
            YS[s, :, half * WID : (half + 1) * WID] = dot(SM[s], held).astype(BF16)
        TK[s, 0:SLOTS, WID : 3 * WID] = YS[s, 0:SLOTS]

    def deliver(s):
        sent = []
        for k in range(1, 8):
            group = pl.ds(k * SLOTS, SLOTS)
            sent.append(send(YS.at[s, group], TK.at[s, group, pl.ds(WID, 2 * WID)], at_yc(k)))
        dispatch.append(sent)

    for copy in second[0]:
        copy.wait_recv()
    select(0)
    deliver(0)

    gates = dot(info, picks, NT)
    count = dot(after, jnp.where(gates > 0.0, 1.0, 0.0).astype(BF16))
    base = (iota((ALL, 128), 0) // BOTH * CAP + iota((ALL, 128), 1) * SLOTS).astype(F32)
    target = jnp.where(gates > 0.0, count + base, -1.0)
    column = iota((8 * TOK, ROWS), 1).astype(F32)
    for s in range(2):
        part = lambda v: v.reshape(8, BOTH, 128)[:, s * TOK : (s + 1) * TOK].reshape(8 * TOK, 128)
        aim, value = part(target), part(gates)
        for n in range(2):
            total = jnp.zeros((8 * TOK, ROWS), F32)
            for k in range(8):
                hit = column == aim[:, k : k + 1]
                total = jnp.where(hit, value[:, 8 * n + k : 8 * n + k + 1], total)
            CM[s, n] = total.astype(BF16)

    for copy in second[1]:
        copy.wait_recv()
    select(1)

    shared = []

    def share(s):
        sent = []
        for group in range(4):
            for k in (2 * group, 2 * group + 1):
                if k > 0:
                    dispatch[s][k - 1].wait_recv()
            rows = pl.ds(2 * group * SLOTS, 2 * SLOTS)
            for m, to, who in ((1, 0, xa), (2, 3, xb)):
                src = TK.at[s, rows, pl.ds(m * WID, WID)]
                sent.append(send(src, TK.at[s, rows, pl.ds(to * WID, WID)], at_x(who)))
        shared.append(sent)

    partial, crossed, around, passed = {}, {}, {}, {}
    other = lax.rem(d + 4, 8)

    def sums(s):
        for copy in shared[s]:
            copy.wait_recv()
        if s == 0:
            for copy in weights:
                copy.wait_recv()
        for c in CHUNKS[s]:
            partial[s, c] = []
            lanes = pl.ds(c[0], c[1] - c[0])
            for n, (w, start, who) in enumerate(((WA, 2 * WID, xa), (WB, 0, xb))):
                rows = TK[s, c[0] : c[1], start : start + 2 * WID]
                PS[s, n, :, c[0] : c[1]] = dot(w[...], rows, NT).astype(BF16)
                partial[s, c].append(send(PS.at[s, n, :, lanes], PR.at[s, n, :, lanes], at_x(who)))
        if s == 0:
            for copy in local[6:]:
                copy.wait()
        PO[s] = dot(WO[...], TK[s], NT)

    def held(s, c, block):
        return HT.at[s, block, :, pl.ds(c[0], c[1] - c[0])]

    def move(s, c, block, who):
        return send(held(s, c, block), held(s, c, block), who)

    def hidden(s, c):
        for copy in partial[s, c]:
            copy.wait_recv()
        both = PO[s, :, c[0] : c[1]]
        for n in range(2):
            both = both + PR[s, n, :, c[0] : c[1]].astype(F32)
        gate, up = both[:HID], both[HID:]
        HT[s, d, :, c[0] : c[1]] = (gate / (1.0 + jnp.exp(-gate)) * up).astype(BF16)
        crossed[s, c] = move(s, c, d, at_z(8))

    def go_round(s, c):
        around[s, c] = [move(s, c, d, at_x(place)) for place in (xa, xb)]

    def relay(s, c):
        around[s, c][0].wait_recv()
        around[s, c].append(move(s, c, zh * 4 + xa, at_x(xb)))

    def pass_on(s, c):
        crossed[s, c].wait_recv()
        passed[s, c] = [move(s, c, other, at_x(place)) for place in (xa, xb)]

    def pass_relay(s, c):
        passed[s, c][1].wait_recv()
        passed[s, c].append(move(s, c, 4 - zh * 4 + xb, at_x(xa)))

    def add(s, c, start):
        @pl.loop(0, 4)
        def _(n):
            w = DW[pl.ds(pl.multiple_of((start + n) * HID, HID), HID), :]
            OA[s, c[0] : c[1]] += dot(HT[s, start + n, :, c[0] : c[1]], w, TN)

    def project_own(s, c):
        for copy in around[s, c][1:]:
            copy.wait_recv()
        OA[s, c[0] : c[1]] = jnp.zeros((c[1] - c[0], WID), F32)
        add(s, c, zh * 4)

    returned = ([], [])

    def project(s, c):
        for copy in (passed[s, c][0], passed[s, c][2]):
            copy.wait_recv()
        add(s, c, 4 - zh * 4)
        OS[s, c[0] : c[1]] = OA[s, c[0] : c[1]].astype(BF16)
        for k in range(c[0] // SLOTS, c[1] // SLOTS):
            group = pl.ds(k * SLOTS, SLOTS)
            if k == 0:
                OB[s, 0:SLOTS] = OS[s, 0:SLOTS]
            else:
                returned[s].append(send(OS.at[s, group], OB.at[s, group], at_yc(-k)))

    last = []

    def combine(s):
        for copy in returned[s]:
            copy.wait_recv()
        rows_in = OB[s]
        total = (dot(CM[s, 0], rows_in) + dot(CM[s, 1], rows_in)).reshape(8, TOK, WID)
        for n in range(4):
            ZF[s, :, n * TOK : (n + 1) * TOK] = total[:, :, n * 128 : (n + 1) * 128]
        ZS[s] = ZF[s].astype(BF16)
        sent = []
        for k in range(1, 8):
            block = k % 4 * 2 + lax.rem(zl + k, 8) // 4
            sent.append(send(ZS.at[s, block], ZR.at[s, k], at_zl(k)))
        last.append(sent)

    def finish(s, out):
        for copy in last[s]:
            copy.wait_recv()
        total = ZF[s, ql]
        for k in range(1, 8):
            total = total + ZR[s, k].astype(F32)
        for n in range(4):
            out[:, n * 128 : (n + 1) * 128] = total[n * TOK : (n + 1) * TOK].astype(BF16)

    (one,), (two, three) = CHUNKS
    share(0)
    deliver(1)
    sums(0)
    share(1)
    hidden(0, one)
    go_round(0, one)
    sums(1)
    relay(0, one)
    hidden(1, two)
    go_round(1, two)
    hidden(1, three)
    go_round(1, three)
    pass_on(0, one)
    project_own(0, one)
    relay(1, two)
    relay(1, three)
    pass_relay(0, one)
    pass_on(1, two)
    project(0, one)
    pass_on(1, three)
    pass_relay(1, two)
    project_own(1, two)
    project_own(1, three)
    pass_relay(1, three)
    project(1, two)
    combine(0)
    project(1, three)
    combine(1)
    finish(0, out1)
    finish(1, out2)
    for copy in copies:
        copy.wait_send()
    assert len(copies) == COPIES


def body(tok1, gat1, exp1, tok2, gat2, exp2, gate_w, up_w, down_w):
    vmem = pl.BlockSpec(memory_space=pltpu.VMEM)
    hbm = pl.BlockSpec(memory_space=pl.ANY)
    scratch = [
        pltpu.VMEM((2, TOK, WID), BF16),
        pltpu.VMEM((2, 8, TOK), F32),
        pltpu.VMEM((2, 8, TOK), jnp.int32),
        pltpu.VMEM((4, 4, BOTH, WID), BF16),
        pltpu.VMEM((4, 2, BOTH, 128), BF16),
        pltpu.VMEM((2, ROWS, 8 * HEAD), BF16),
        pltpu.VMEM((2, ROWS, 2 * WID), BF16),
        pltpu.VMEM((2, ROWS, 4 * WID), BF16),
        pltpu.VMEM((2 * HID, 4 * WID), BF16),
        pltpu.VMEM((2 * HID, 2 * WID), BF16),
        pltpu.VMEM((2 * HID, 2 * WID), BF16),
        pltpu.VMEM((8 * HID, WID), BF16),
        pltpu.VMEM((2, 2, 2 * HID, ROWS), BF16),
        pltpu.VMEM((2, 2, 2 * HID, ROWS), BF16),
        pltpu.VMEM((2, 2 * HID, ROWS), F32),
        pltpu.VMEM((2, 8, HID, ROWS), BF16),
        pltpu.VMEM((2, ROWS, WID), F32),
        pltpu.VMEM((2, ROWS, WID), BF16),
        pltpu.VMEM((2, ROWS, WID), BF16),
        pltpu.VMEM((2, 2, 8 * TOK, ROWS), BF16),
        pltpu.VMEM((2, 8, 4 * TOK, 128), F32),
        pltpu.VMEM((2, 8, 4 * TOK, 128), BF16),
        pltpu.VMEM((2, 8, 4 * TOK, 128), BF16),
        pltpu.SemaphoreType.DMA((COPIES,)),
        pltpu.SemaphoreType.DMA((COPIES,)),
        pltpu.SemaphoreType.DMA((15,)),
    ]
    result = jax.ShapeDtypeStruct((TOK, WID), BF16)
    return pl.pallas_call(
        kernel,
        out_shape=(result, result),
        in_specs=[hbm] * 9,
        out_specs=(vmem, vmem),
        scratch_shapes=scratch,
        compiler_params=pltpu.CompilerParams(
            collective_id=0, has_side_effects=True, vmem_limit_bytes=60 * 2**20
        ),
        cost_estimate=pl.CostEstimate(
            flops=2 * 2 * ROWS * (2 * HID * 4096 + 1536 * WID),
            bytes_accessed=3 * HID * 4096 * 2,
            transcendentals=2 * HID * ROWS,
        ),
        name="moe",
    )(tok1, gat1.T, exp1.T, tok2, gat2.T, exp2.T, gate_w, up_w, down_w)


def solution(mesh):
    return jax.shard_map(
        body,
        mesh=mesh,
        in_specs=(
            P("expert", "dp"),
            P("expert", None),
            P("expert", None),
            P("expert", "dp"),
            P("expert", None),
            P("expert", None),
            P("expert", "dp", None),
            P("expert", "dp", None),
            P("expert", None, "dp"),
        ),
        out_specs=(P("expert", "dp"), P("expert", "dp")),
        check_vma=False,
    )
```

time: 144 us -> 130 us (0.903)
  local copies, waits for them, and re-layouts: 9.95 us -> 2.69 us
  Pallas kernels: 133 us -> 126 us
    unnamed x16 -> x2, local copies, waits for them, and re-layouts: 9.95 us -> 2.69 us
    pallas_call x1, Pallas kernels: 133 us -> 126 us  [body(): pl.pallas_call(kernel, out_shape=(result, result), in_specs=[hbm] * 9, ou...]
where the time goes in v2:
time: 130 us; the launch traced here: 129 us
  Pallas kernels  126 us (97%)
  local copies, waits for them, and re-layouts  2.69 us (2%)
    pallas_call x1, Pallas kernels, body(): pl.pallas_call(kernel, out_shape=(result, result), in_specs=[hbm] * 9, ou...  126 us
    unnamed x2, local copies, waits for them, and re-layouts  2.69 us

profile of v2, /device:TPU:1, one launch (start us, length us, event | category | flops | bytes accessed | tf_op | source)
XLA Modules:
  0.0 128.9 jit_solution(14211996647878000524)
XLA Ops:
  0.6 125.5 %moe.1 = (bf16[24,512]{1,0:T(8,128)(2,1)}, bf16[24,512]{1,0:T(8,128)(2,1)}) custom-call(bf16[24,512]{1,0:T(8,128)(2,1)} %tok1.1, f32[8,24]{1,0:T(8,128)} %bitcast.4, s32[8,24]{1,0:T(8,128)} %bitcast.5, bf16[24,512]{1,0:T(8,128)(2,1)} %tok2.1, f32[8,24]{1,0:T(8,128)} %bitcast.6, s32[8,24]{1,0:T(8,128)} %bitcast.7, bf16[1,192,4096]{2,1,0:T(8,128)(2,1)} %gate_w.1, ...), custom_call_target="tpu_custom_call" | custom-call | flops 3623878656 | bytes 4718592 | tf_op jit(solution)/shard_map/moe/pallas_call | solution.py:415
  126.2 1.3 %copy.13 = bf16[24,512]{1,0:T(8,128)(2,1)} copy(bf16[24,512]{1,0:T(8,128)(2,1)} %get-tuple-element.4) | data formatting | bytes 49152
  127.5 1.3 %copy.14 = bf16[24,512]{1,0:T(8,128)(2,1)} copy(bf16[24,512]{1,0:T(8,128)(2,1)} %get-tuple-element.5) | data formatting | bytes 49152

commit v3 on v2

--- a/solution.py
+++ b/solution.py
@@ -279,7 +279,7 @@
         crossed[s, c] = move(s, c, d, at_z(8))
 
     def go_round(s, c):
-        around[s, c] = [move(s, c, d, at_x(place)) for place in (xa, xb)]
+        around[s, c] = [move(s, c, d, at_x(place)) for place in ((xa, xb, xc) if c[1] - c[0] == 128 else (xa, xb))]
 
     def relay(s, c):
         around[s, c][0].wait_recv()
@@ -287,7 +287,8 @@
 
     def pass_on(s, c):
         crossed[s, c].wait_recv()
-        passed[s, c] = [move(s, c, other, at_x(place)) for place in (xa, xb)]
+        places = (xa, xb, xc) if c[1] - c[0] == 128 else (xa, xb)
+        passed[s, c] = [move(s, c, other, at_x(place)) for place in places]
 
     def pass_relay(s, c):
         passed[s, c][1].wait_recv()
@@ -300,7 +301,7 @@
             OA[s, c[0] : c[1]] += dot(HT[s, start + n, :, c[0] : c[1]], w, TN)
 
     def project_own(s, c):
-        for copy in around[s, c][1:]:
+        for copy in around[s, c][0 if c[1] - c[0] == 128 else 1 :]:
             copy.wait_recv()
         OA[s, c[0] : c[1]] = jnp.zeros((c[1] - c[0], WID), F32)
         add(s, c, zh * 4)
@@ -308,8 +309,8 @@
     returned = ([], [])
 
     def project(s, c):
-        for copy in (passed[s, c][0], passed[s, c][2]):
-            copy.wait_recv()
+        for n in (0, 1, 2) if c[1] - c[0] == 128 else (0, 2):
+            passed[s, c][n].wait_recv()
         add(s, c, 4 - zh * 4)
         OS[s, c[0] : c[1]] = OA[s, c[0] : c[1]].astype(BF16)
         for k in range(c[0] // SLOTS, c[1] // SLOTS):
@@ -360,7 +361,6 @@
     pass_on(0, one)
     project_own(0, one)
     relay(1, two)
-    relay(1, three)
     pass_relay(0, one)
     pass_on(1, two)
     project(0, one)
@@ -368,7 +368,6 @@
     pass_relay(1, two)
     project_own(1, two)
     project_own(1, three)
-    pass_relay(1, three)
     project(1, two)
     combine(0)
     project(1, three)

time: 130 us -> 131 us (level)
  the two profiles are of different devices: /device:TPU:1 before, /device:TPU:10 now
where the time goes in v3:
time: 131 us
  Pallas kernels  127 us (97%)
  local copies, waits for them, and re-layouts  2.69 us (2%)
    pallas_call x1, Pallas kernels, body(): pl.pallas_call(kernel, out_shape=(result, result), in_specs=[hbm] * 9, ou...  127 us
    unnamed x2, local copies, waits for them, and re-layouts  2.69 us

profile of v3, /device:TPU:10, one launch (start us, length us, event | category | flops | bytes accessed | tf_op | source)
XLA Modules:
  0.0 130.8 jit_solution(13671052075158583955)
XLA Ops:
  0.6 127.4 %moe.1 = (bf16[24,512]{1,0:T(8,128)(2,1)}, bf16[24,512]{1,0:T(8,128)(2,1)}) custom-call(bf16[24,512]{1,0:T(8,128)(2,1)} %tok1.1, f32[8,24]{1,0:T(8,128)} %bitcast.4, s32[8,24]{1,0:T(8,128)} %bitcast.5, bf16[24,512]{1,0:T(8,128)(2,1)} %tok2.1, f32[8,24]{1,0:T(8,128)} %bitcast.6, s32[8,24]{1,0:T(8,128)} %bitcast.7, bf16[1,192,4096]{2,1,0:T(8,128)(2,1)} %gate_w.1, ...), custom_call_target="tpu_custom_call" | custom-call | flops 3623878656 | bytes 4718592 | tf_op jit(solution)/shard_map/moe/pallas_call | solution.py:414
  128.1 1.3 %copy.13 = bf16[24,512]{1,0:T(8,128)(2,1)} copy(bf16[24,512]{1,0:T(8,128)(2,1)} %get-tuple-element.4) | data formatting | bytes 49152
  129.4 1.3 %copy.14 = bf16[24,512]{1,0:T(8,128)(2,1)} copy(bf16[24,512]{1,0:T(8,128)(2,1)} %get-tuple-element.5) | data formatting | bytes 49152

commit v4 on v2

--- a/solution.py
+++ b/solution.py
@@ -358,19 +358,19 @@
     hidden(1, three)
     go_round(1, three)
     pass_on(0, one)
-    project_own(0, one)
     relay(1, two)
     relay(1, three)
+    project_own(0, one)
     pass_relay(0, one)
+    project(0, one)
     pass_on(1, two)
-    project(0, one)
     pass_on(1, three)
+    combine(0)
     pass_relay(1, two)
     project_own(1, two)
     project_own(1, three)
     pass_relay(1, three)
     project(1, two)
-    combine(0)
     project(1, three)
     combine(1)
     finish(0, out1)

time: 130 us -> 133 us (1.023)
  Pallas kernels: 126 us -> 128 us
    pallas_call x1, Pallas kernels: 126 us -> 128 us  [body(): pl.pallas_call(kernel, out_shape=(result, result), in_specs=[hbm] * 9, ou...]
where the time goes in v4:
time: 133 us; the launch traced here: 131 us
  Pallas kernels  128 us (96%)
  local copies, waits for them, and re-layouts  2.69 us (2%)
    pallas_call x1, Pallas kernels, body(): pl.pallas_call(kernel, out_shape=(result, result), in_specs=[hbm] * 9, ou...  128 us
    unnamed x2, local copies, waits for them, and re-layouts  2.69 us

profile of v4, /device:TPU:1, one launch (start us, length us, event | category | flops | bytes accessed | tf_op | source)
XLA Modules:
  0.0 131.4 jit_solution(14032000443676571503)
XLA Ops:
  0.6 128.1 %moe.1 = (bf16[24,512]{1,0:T(8,128)(2,1)}, bf16[24,512]{1,0:T(8,128)(2,1)}) custom-call(bf16[24,512]{1,0:T(8,128)(2,1)} %tok1.1, f32[8,24]{1,0:T(8,128)} %bitcast.4, s32[8,24]{1,0:T(8,128)} %bitcast.5, bf16[24,512]{1,0:T(8,128)(2,1)} %tok2.1, f32[8,24]{1,0:T(8,128)} %bitcast.6, s32[8,24]{1,0:T(8,128)} %bitcast.7, bf16[1,192,4096]{2,1,0:T(8,128)(2,1)} %gate_w.1, ...), custom_call_target="tpu_custom_call" | custom-call | flops 3623878656 | bytes 4718592 | tf_op jit(solution)/shard_map/moe/pallas_call | solution.py:415
  128.7 1.3 %copy.13 = bf16[24,512]{1,0:T(8,128)(2,1)} copy(bf16[24,512]{1,0:T(8,128)(2,1)} %get-tuple-element.4) | data formatting | bytes 49152
  130.1 1.3 %copy.14 = bf16[24,512]{1,0:T(8,128)(2,1)} copy(bf16[24,512]{1,0:T(8,128)(2,1)} %get-tuple-element.5) | data formatting | bytes 49152
